TPU v7x, 32 devices: a whole 2x2x4 slice. The times are simulated.
32 devices in a mesh: dp: 2 (over x), ctx: 8 (over z, core), head: 2 (over y).
Axes of the slice: x: 2, y: 2, z: 4, core: 2. Of those that a mesh axis runs over, the one named last changes fastest.
Arguments:
- queries: bfloat16 [1024, 4, 1024], P('ctx', ('dp', 'head')), may hold values from -5 to 5
- keys: bfloat16 [1024, 4, 128], P(('ctx', 'head', 'dp')), may hold values from -5 to 5
- values: bfloat16 [1024, 4, 128], P(('ctx', 'head', 'dp')), may hold values from -6 to 6
- outputs: bfloat16 [1024, 4, 1024], P('ctx', ('dp', 'head')), may hold values from -3 to 3
- grad_out: bfloat16 [1024, 4, 1024], P('ctx', ('dp', 'head')), may hold values from -6 to 6
- doc_ids: int32 [1024], P('ctx'), may hold values from 0 to 3, never falling along the last dimension, each value on 1 to 512 neighbouring positions
- owner: int32 [32], P('ctx'), may hold values from 0 to 7, as said below
Outputs:
- grad_q_planned: bfloat16 [1024, 4, 1024], P('ctx', ('dp', 'head'))
- grad_k: bfloat16 [1024, 4, 128], P('ctx', ('dp', 'head'))
- grad_v: bfloat16 [1024, 4, 128], P('ctx', ('dp', 'head'))
Inputs may be any that keep to these rules, and one draw needn't show every extreme that they name: `owner`: blocks b with the same b // 4 have different owners, and blocks with the same b % 4 have different owners, so every index of ctx owns exactly 4 blocks, one for each value of b % 4.
All inputs are finite; a program needn't handle non-finite values.
Results may differ from a plain program's by a relative error of at most 0.0047.
The roundings to bfloat16 on the way count: a program that leaves them out, or rounds other values in their place, can miss the bound.
Values may be sent and summed in bfloat16 or wider, within the bound.
A program may use at most 64 MiB of HBM per device.

v0:
```python
import jax
import jax.numpy as jnp
from jax import lax
from jax.sharding import PartitionSpec as P

NEG_FILL = -1e30


def as_heads(block, head_dim):
    return block.reshape(block.shape[0], block.shape[1], block.shape[2] // head_dim, head_dim)


def visible_mask(q_pos, q_doc, key_start, key_doc):
    key_pos = key_start + jnp.arange(key_doc.shape[0], dtype=jnp.int32)
    return (key_doc[None, :] == q_doc[:, None]) & (key_pos[None, :] <= q_pos[:, None])


def raw_scores(q_heads, key_block, scale_val):
    return (
        jnp.einsum("rgid,kgd->girk", q_heads, key_block, preferred_element_type=jnp.float32)
        * scale_val
    )


def softmax_totals(q_heads, all_keys, all_docs, q_pos, q_doc, scale_val, key_step):
    last_query = jnp.max(q_pos)
    shape = (q_heads.shape[1], q_heads.shape[2], q_heads.shape[0])

    def visit(block_index, state):
        key_start = block_index * key_step

        def work(inner):
            peak, total = inner
            key_block = lax.dynamic_slice_in_dim(all_keys, key_start, key_step, 0)
            key_doc = lax.dynamic_slice_in_dim(all_docs, key_start, key_step, 0)
            visible = visible_mask(q_pos, q_doc, key_start, key_doc)[None, None]
            scores = raw_scores(q_heads, key_block, scale_val)
            fresh = jnp.maximum(peak, jnp.max(jnp.where(visible, scores, NEG_FILL), axis=-1))
            weights = jnp.where(visible, jnp.exp(scores - fresh[..., None]), 0.0)
            return (fresh, total * jnp.exp(peak - fresh) + jnp.sum(weights, axis=-1))

        return lax.cond(key_start <= last_query, work, lambda inner: inner, state)

    start_state = (jnp.full(shape, NEG_FILL, jnp.float32), jnp.zeros(shape, jnp.float32))
    peak, total = lax.fori_loop(0, all_keys.shape[0] // key_step, visit, start_state)
    return peak + jnp.log(total)


def block_terms(
    q_heads,
    do_heads,
    key_block,
    value_block,
    key_start,
    key_doc,
    q_pos,
    q_doc,
    lse,
    delta,
    scale_val,
):
    visible = visible_mask(q_pos, q_doc, key_start, key_doc)[None, None]
    scores = raw_scores(q_heads, key_block, scale_val)
    probs = jnp.where(visible, jnp.exp(scores - lse[..., None]), 0.0)
    dprob = jnp.einsum("rgid,kgd->girk", do_heads, value_block, preferred_element_type=jnp.float32)
    dscore = (probs * (dprob - delta[..., None]) * scale_val).astype(jnp.bfloat16)
    return (probs.astype(jnp.bfloat16), dscore)


def body(queries, keys, values, outputs, grad_out, doc_ids, owner):
    head_dim = keys.shape[2]
    scale_val = head_dim ** (-0.5)
    row_count = queries.shape[0]
    peer_count = lax.axis_size("ctx")
    per_device = owner.shape[0]
    block_len = row_count // per_device
    near_keys, near_values = (
        lax.all_to_all(
            lax.all_to_all(keys, "dp", split_axis=1, concat_axis=0, tiled=True),
            "head",
            split_axis=1,
            concat_axis=0,
            tiled=True,
        ),
        lax.all_to_all(
            lax.all_to_all(values, "dp", split_axis=1, concat_axis=0, tiled=True),
            "head",
            split_axis=1,
            concat_axis=0,
            tiled=True,
        ),
    )
    all_keys, all_values, all_docs = (
        lax.all_gather(near_keys, "ctx", axis=0, tiled=True),
        lax.all_gather(near_values, "ctx", axis=0, tiled=True),
        lax.all_gather(doc_ids, "ctx", axis=0, tiled=True),
    )
    total_len = all_keys.shape[0]
    kv_local = all_keys.shape[1]
    key_step = min(512, total_len)
    slot_ids = jnp.arange(per_device, dtype=jnp.int32)
    peer_ids = jnp.arange(peer_count, dtype=jnp.int32)
    send_hot = owner[None, :] == peer_ids[:, None]
    send_tag = jnp.sum(jnp.where(send_hot, slot_ids[None, :] + 1, 0), axis=1, keepdims=True)
    send_mat = send_hot.astype(jnp.bfloat16)
    q_rows, do_rows, o_rows = (queries, grad_out, outputs)
    q_pos = lax.axis_index("ctx") * row_count + jnp.arange(row_count, dtype=jnp.int32)
    q_doc = jnp.take(all_docs, q_pos)
    q_heads = as_heads(q_rows, head_dim)
    do_heads = as_heads(do_rows, head_dim)
    o_heads = as_heads(o_rows, head_dim)
    delta = jnp.transpose(
        jnp.sum(do_heads.astype(jnp.float32) * o_heads.astype(jnp.float32), axis=-1), (1, 2, 0)
    )
    lse = softmax_totals(q_heads, all_keys, all_docs, q_pos, q_doc, scale_val, key_step)
    last_query = jnp.max(q_pos)

    def grads_at(key_start, size):
        key_block = lax.dynamic_slice_in_dim(all_keys, key_start, size, 0)
        value_block = lax.dynamic_slice_in_dim(all_values, key_start, size, 0)
        key_doc = lax.dynamic_slice_in_dim(all_docs, key_start, size, 0)
        probs_low, dscore = block_terms(
            q_heads,
            do_heads,
            key_block,
            value_block,
            key_start,
            key_doc,
            q_pos,
            q_doc,
            lse,
            delta,
            scale_val,
        )
        return (key_block, probs_low, dscore)

    def key_grads(probs_low, dscore):
        dk_block = jnp.einsum("girk,rgid->kgd", dscore, q_heads, preferred_element_type=jnp.float32)
        dv_block = jnp.einsum(
            "girk,rgid->kgd", probs_low, do_heads, preferred_element_type=jnp.float32
        )
        return jnp.concatenate([dk_block, dv_block], axis=-1)

    def query_grads(dscore, key_block):
        return jnp.einsum("girk,kgd->rgid", dscore, key_block, preferred_element_type=jnp.float32)

    dq_zero = jnp.zeros(q_heads.shape, jnp.float32)

    def visit_all(block_index, state):
        key_start = block_index * key_step

        def work(inner):
            dq_sum, key_sum = inner
            key_block, probs_low, dscore = grads_at(key_start, key_step)
            dq_sum = dq_sum + query_grads(dscore, key_block)
            key_sum = lax.dynamic_update_slice_in_dim(
                key_sum, key_grads(probs_low, dscore), key_start, 0
            )
            return (dq_sum, key_sum)

        return lax.cond(key_start <= last_query, work, lambda inner: inner, state)

    key_zero = jnp.zeros((total_len, kv_local, 2 * head_dim), jnp.float32)
    dq_sum, key_sum = lax.fori_loop(0, total_len // key_step, visit_all, (dq_zero, key_zero))
    combined = lax.psum_scatter(key_sum, "ctx", scatter_dimension=0, tiled=True)
    dq_low = dq_sum.reshape(row_count, kv_local, -1).astype(jnp.bfloat16)
    blocks = dq_low.reshape((per_device, block_len) + dq_low.shape[1:])
    dq_recv = lax.all_to_all(
        jnp.einsum("pj,jbgw->pbgw", send_mat, blocks, preferred_element_type=jnp.float32).astype(
            jnp.bfloat16
        ),
        "ctx",
        split_axis=0,
        concat_axis=0,
        tiled=True,
    )
    tag_recv = lax.all_to_all(send_tag, "ctx", split_axis=0, concat_axis=0, tiled=True)
    pick_hot = tag_recv[:, 0][None, :] == slot_ids[:, None] + 1
    pick_hot, pick_mat = (pick_hot, pick_hot.astype(jnp.bfloat16))
    placed = jnp.einsum(
        "jp,pbgw->jbgw", pick_mat, dq_recv, preferred_element_type=jnp.float32
    ).astype(jnp.bfloat16)
    dq_out = placed.reshape((row_count,) + dq_recv.shape[2:])
    grad_k = combined[..., :head_dim].astype(jnp.bfloat16)
    grad_v = combined[..., head_dim:].astype(jnp.bfloat16)
    return (dq_out, grad_k, grad_v)


def solution(mesh):
    placed = (
        P("ctx", ("dp", "head"), None),
        P(("ctx", "head", "dp"), None, None),
        P(("ctx", "head", "dp"), None, None),
        P("ctx", ("dp", "head"), None),
        P("ctx", ("dp", "head"), None),
        P("ctx"),
        P("ctx"),
    )
    return jax.shard_map(
        body,
        mesh=mesh,
        in_specs=placed,
        out_specs=(
            P("ctx", ("dp", "head"), None),
            P("ctx", ("dp", "head"), None),
            P("ctx", ("dp", "head"), None),
        ),
        check_vma=False,
    )
```

profile of v0, /device:TPU:0, one launch (start us, length us, event | category | flops | bytes accessed | tf_op | source)
XLA Modules:
  0.0 127.8 jit_solution(6998216010043129332)
XLA Ops:
  7.2 1.4 %copy.85 = bf16[32,4,128]{2,0,1:T(8,128)(2,1)} copy(bf16[32,4,128]{2,1,0:T(4,128)(2,1)} %param.16) | data formatting | bytes 65536 | tf_op args[1]
  8.6 4.2 %all-to-all-start.1 = ((bf16[32,4,128]{2,0,1:T(8,128)(2,1)}), bf16[32,4,128]{2,0,1:T(8,128)(2,1)S(1)}, u32[]{:S(2)}, u32[]{:S(2)}) async-start(bf16[32,4,128]{2,0,1:T(8,128)(2,1)} %copy.85), calls=%async_computation.1 | async-start | bytes 65536 | tf_op jit(solution)/shard_map/all_to_all | solution.py:79
  12.8 1.4 %copy.89 = bf16[32,4,128]{2,0,1:T(8,128)(2,1)} copy(bf16[32,4,128]{2,1,0:T(4,128)(2,1)} %param.17) | data formatting | bytes 65536 | tf_op args[2]
  14.2 12.6 %all-gather = s32[8,1,128]{2,1,0:T(1,128)S(1)} all-gather(s32[1,1,128]{2,1,0:T(1,128)} %bitcast.163), channel_id=1, replica_groups=mesh['dp'=2,'ctx'=8,'head'=2] {'ctx'}, dimensions={0}, use_global_device_ids=true | all-gather | bytes 4608 | tf_op jit(solution)/shard_map/all_gather | solution.py:96
  26.8 1.0 gather_fusion
  27.8 3.3 %all-to-all-start.3 = ((bf16[32,4,128]{2,0,1:T(8,128)(2,1)}), bf16[32,4,128]{2,0,1:T(8,128)(2,1)S(1)}, u32[]{:S(2)}, u32[]{:S(2)}) async-start(bf16[32,4,128]{2,0,1:T(8,128)(2,1)} %copy.89), calls=%async_computation.3 | async-start | bytes 65536 | tf_op jit(solution)/shard_map/all_to_all | solution.py:86
  31.1 1.1 copy.91
  32.2 1.1 copy.92
  33.3 0.6 copy.86
  33.9 1.1 all-to-all-done.3
  35.0 3.3 %all-to-all-start.2 = ((bf16[64,2,128]{2,0,1:T(8,128)(2,1)}), bf16[64,2,128]{2,0,1:T(8,128)(2,1)S(1)}, u32[]{:S(2)}, u32[]{:S(2)}) async-start(bf16[64,2,128]{2,0,1:T(8,128)(2,1)} %bitcast.39), calls=%async_computation.2 | async-start | bytes 65536 | tf_op jit(solution)/shard_map/all_to_all | solution.py:78
  38.4 0.6 fusion.47
  39.0 0.2 copy.87
  39.2 0.2 copy.88
  39.3 0.6 copy.90
  40.0 2.2 %all-to-all-done.2 = bf16[64,2,128]{2,0,1:T(8,128)(2,1)S(1)} async-done(((bf16[64,2,128]{2,0,1:T(8,128)(2,1)}), bf16[64,2,128]{2,0,1:T(8,128)(2,1)S(1)}, u32[]{:S(2)}, u32[]{:S(2)}) %all-to-all-start.2) | async-done | bytes 32800 | tf_op jit(solution)/shard_map/all_to_all | solution.py:78
  42.2 3.3 %all-to-all-start.4 = ((bf16[64,2,128]{2,0,1:T(8,128)(2,1)}), bf16[64,2,128]{2,0,1:T(8,128)(2,1)S(1)}, u32[]{:S(2)}, u32[]{:S(2)}) async-start(bf16[64,2,128]{2,0,1:T(8,128)(2,1)} %bitcast.49), calls=%async_computation.4 | async-start | bytes 65536 | tf_op jit(solution)/shard_map/all_to_all | solution.py:85
  45.5 14.2 %all_gather.9 = bf16[1024,1,128]{2,0,1:T(8,128)(2,1)S(1)} all-gather(bf16[128,1,128]{2,0,1:T(8,128)(2,1)S(1)} %bitcast.158), channel_id=1, replica_groups=mesh['dp'=2,'ctx'=8,'head'=2] {'ctx'}, dimensions={0}, use_global_device_ids=true | all-gather | bytes 294912 | tf_op jit(solution)/shard_map/all_gather | solution.py:94
  59.7 14.2 %all_gather.11 = bf16[1024,1,128]{2,0,1:T(8,128)(2,1)S(1)} all-gather(bf16[128,1,128]{2,0,1:T(8,128)(2,1)S(1)} %bitcast.159), channel_id=1, replica_groups=mesh['dp'=2,'ctx'=8,'head'=2] {'ctx'}, dimensions={0}, use_global_device_ids=true | all-gather | bytes 294912 | tf_op jit(solution)/shard_map/all_gather | solution.py:95
  73.9 2.5 %while.32 = (s32[]{:T(128)}, f32[1,8,128]{2,1,0:T(8,128)S(1)}, f32[1,8,128]{2,1,0:T(8,128)S(1)}, s32[]{:T(128)}, s32[1024]{0:T(1024)S(1)}, /*index=5*/s32[128]{0...) while((s32[]{:T(128)}, f32[1,8,128]{2,1,0:T(8,128)S(1)}, ...), condition=%wide.region_7.8_spmd.clone, body=%wide.region_2.7_spmd.clone.sunk | while | flops 138087040 | bytes 4850473 | solution.py:45
  74.5 1.3 conditional.6
  74.6 0.2 compare_and_fusion
  74.8 0.5 fusion.4
  75.3 0.4 fusion.7
  76.5 0.1 broadcast_in_dim.77
  76.6 3.9 %while.33 = (s32[]{:T(128)}, f32[128,1,8,128]{0,3,2,1:T(8,128)S(1)}, f32[1024,1,256]{0,2,1:T(8,128)S(1)}, s32[]{:T(128)}, bf16[1024,1,128]{2,0,1:T(8,128)(2,1)S(...) while((s32[]{:T(128)}, ...), condition=%wide.region_12.13_spmd.clone, body=%wide.region_9.12_spmd.clone.sunk | while | flops 675742336 | bytes 13652853 | solution.py:164
  77.2 2.7 %conditional.7 = ((f32[128,1,8,128]{0,3,2,1:T(8,128)S(1)}, f32[1024,1,256]{0,2,1:T(8,128)S(1)})) conditional(s32[]{:T(128)} %convert_element_type.101, (f32[128,1,8,128]{0,3,2,1:T(8,128)S(1)}, f32[1024,1,256]{0,2,1:T(8,128)S(1)}) %tuple.92, (s32[]{:T(128)}, bf16[1024,1,128]{2,0,1:T(8,128)(2,1)S(1)}, s32[1024]{0:T(1024)S(1)}, s32[128]{0:T(128)S(1)}, ...), branch_computations={%region_10.10_spmd, %region_11.11_spmd} | conditional | flops 675742336 | bytes 13652054 | solution.py:161
  77.3 0.2 compare_and_fusion.1
  77.5 0.6 fusion.17
  78.0 0.5 convolution_bitcast_fusion.1
  78.5 0.4 fusion.18
  79.0 0.5 convolution_bitcast_fusion.2
  79.5 0.3 fusion.19
  80.5 1.3 %copy.98 = f32[1024,1,256]{2,0,1:T(8,128)} copy(f32[1024,1,256]{0,2,1:T(8,128)S(1)} %get-tuple-element.456) | data formatting | bytes 2097152 | tf_op jit(solution)/shard_map/while | solution.py:164
  82.0 0.7 copy.84
  82.6 5.8 %all-to-all-start = ((s32[8,1,1]{2,1,0:T(1,128)}), s32[8,1,1]{2,1,0:T(1,128)S(1)}, u32[]{:S(2)}, u32[]{:S(2)}) async-start(s32[8,1,1]{2,1,0:T(1,128)} %copy.84), calls=%async_computation | async-start | bytes 8192 | tf_op jit(solution)/shard_map/all_to_all | solution.py:177
  88.5 0.2 copy.93
  88.7 0.1 convert_element_type.79
  88.8 0.4 fusion.35
  89.2 1.1 copy.95
  90.3 3.6 %all-to-all-done = s32[8,1,1]{2,1,0:T(1,128)S(1)} async-done(((s32[8,1,1]{2,1,0:T(1,128)}), s32[8,1,1]{2,1,0:T(1,128)S(1)}, u32[]{:S(2)}, u32[]{:S(2)}) %all-to-all-start) | async-done | bytes 64 | tf_op jit(solution)/shard_map/all_to_all | solution.py:177
  94.0 3.5 %all-to-all-start.5 = ((bf16[8,32,1,1024]{3,1,2,0:T(8,128)(2,1)}), bf16[8,32,1,1024]{3,1,2,0:T(8,128)(2,1)S(1)}, u32[]{:S(2)}, u32[]{:S(2)}) async-start(bf16[8,32,1,1024]{3,1,2,0:T(8,128)(2,1)} %copy.95), calls=%async_computation.5 | async-start | bytes 1048576 | tf_op jit(solution)/shard_map/all_to_all | solution.py:168
  97.5 0.2 reduce.3
  97.7 20.5 %all-to-all-done.5 = bf16[8,32,1,1024]{3,1,2,0:T(8,128)(2,1)S(1)} async-done(((bf16[8,32,1,1024]{3,1,2,0:T(8,128)(2,1)}), bf16[8,32,1,1024]{3,1,2,0:T(8,128)(2,1)S(1)}, u32[]{:S(2)}, u32[]{:S(2)}) %all-to-all-start.5) | async-done | bytes 524320 | tf_op jit(solution)/shard_map/all_to_all | solution.py:168
  118.2 0.4 convolution_convert_fusion.1
  118.7 0.8 copy.97
  119.5 0.9 convert.5
  120.4 0.6 fusion.48
  (36 shorter events, 0.6 us)
Async XLA Ops:
  7.2 31.8 %copy-start = (bf16[128,1,1024]{2,0,1:T(8,128)(2,1)S(1)}, bf16[128,1,1024]{2,0,1:T(8,128)(2,1)}, u32[]{:S(2)}) copy-start(bf16[128,1,1024]{2,0,1:T(8,128)(2,1)} %param.15) | copy-start | bytes 786436
  8.6 19.2 %all-to-all-start.1 = ((bf16[32,4,128]{2,0,1:T(8,128)(2,1)}), bf16[32,4,128]{2,0,1:T(8,128)(2,1)S(1)}, u32[]{:S(2)}, u32[]{:S(2)}) async-start(bf16[32,4,128]{2,0,1:T(8,128)(2,1)} %copy.85), calls=%async_computation.1 | async-start | bytes 65536 | tf_op jit(solution)/shard_map/all_to_all | solution.py:79
  27.8 7.2 %all-to-all-start.3 = ((bf16[32,4,128]{2,0,1:T(8,128)(2,1)}), bf16[32,4,128]{2,0,1:T(8,128)(2,1)S(1)}, u32[]{:S(2)}, u32[]{:S(2)}) async-start(bf16[32,4,128]{2,0,1:T(8,128)(2,1)} %copy.89), calls=%async_computation.3 | async-start | bytes 65536 | tf_op jit(solution)/shard_map/all_to_all | solution.py:86
  35.0 7.2 %all-to-all-start.2 = ((bf16[64,2,128]{2,0,1:T(8,128)(2,1)}), bf16[64,2,128]{2,0,1:T(8,128)(2,1)S(1)}, u32[]{:S(2)}, u32[]{:S(2)}) async-start(bf16[64,2,128]{2,0,1:T(8,128)(2,1)} %bitcast.39), calls=%async_computation.2 | async-start | bytes 65536 | tf_op jit(solution)/shard_map/all_to_all | solution.py:78
  42.2 17.5 %all-to-all-start.4 = ((bf16[64,2,128]{2,0,1:T(8,128)(2,1)}), bf16[64,2,128]{2,0,1:T(8,128)(2,1)S(1)}, u32[]{:S(2)}, u32[]{:S(2)}) async-start(bf16[64,2,128]{2,0,1:T(8,128)(2,1)} %bitcast.49), calls=%async_computation.4 | async-start | bytes 65536 | tf_op jit(solution)/shard_map/all_to_all | solution.py:85
  45.5 74.0 %reduce-scatter.2.cloned.1.call-start = ((), (), s32[]{:S(2)}) async-start(), calls=%async_computation.7 | async-start | bytes 1179648 | tf_op jit(solution)/shard_map/reduce_scatter | solution.py:165
  80.5 1.4 %copy-start.1 = (s32[4]{0:T(128)S(1)}, s32[4]{0:T(128)}, u32[]{:S(2)}) copy-start(s32[4]{0:T(128)} %param.21) | copy-start | bytes 52
  82.6 11.3 %all-to-all-start = ((s32[8,1,1]{2,1,0:T(1,128)}), s32[8,1,1]{2,1,0:T(1,128)S(1)}, u32[]{:S(2)}, u32[]{:S(2)}) async-start(s32[8,1,1]{2,1,0:T(1,128)} %copy.84), calls=%async_computation | async-start | bytes 8192 | tf_op jit(solution)/shard_map/all_to_all | solution.py:177
  94.0 24.3 %all-to-all-start.5 = ((bf16[8,32,1,1024]{3,1,2,0:T(8,128)(2,1)}), bf16[8,32,1,1024]{3,1,2,0:T(8,128)(2,1)S(1)}, u32[]{:S(2)}, u32[]{:S(2)}) async-start(bf16[8,32,1,1024]{3,1,2,0:T(8,128)(2,1)} %copy.95), calls=%async_computation.5 | async-start | bytes 1048576 | tf_op jit(solution)/shard_map/all_to_all | solution.py:168
Sparse Core Ops, SparseCore 0:
  82.0 36.4 reduce-scatter.1
where the time goes:
time: 129 us; the launch traced here: 128 us
  blocking collectives  41 us (32%)
  waiting for transfers between devices  27.5 us (21%)
  starting transfers between devices  23.4 us (18%)
  between operations  14.2 us (11%)
  local copies, waits for them, and re-layouts  12.7 us (10%)
  matrix products  3.6 us (3%)
  other arithmetic  2.93 us (2%)
  loops' own time  2.55 us (2%)
    all_to_all x1, waiting for transfers between devices, body(): lax.all_to_all(jnp.einsum('pj,jbgw->pbgw', send_mat, blocks, preferred_el...  20.5 us
    all_gather x1, blocking collectives, body(): lax.all_gather(near_values, 'ctx', axis=0, tiled=True)  14.2 us
    all_gather x1, blocking collectives, body(): lax.all_gather(near_keys, 'ctx', axis=0, tiled=True)  14.2 us
    all_gather x1, blocking collectives, body(): lax.all_gather(doc_ids, 'ctx', axis=0, tiled=True)  12.6 us
    all_to_all x1, starting transfers between devices, body(): lax.all_to_all(send_tag, 'ctx', split_axis=0, concat_axis=0, tiled=True)  5.83 us
    unnamed x9, local copies, waits for them, and re-layouts  4.29 us
    all_to_all x1, starting transfers between devices, body(): lax.all_to_all(keys, 'dp', split_axis=1, concat_axis=0, tiled=True)  4.21 us
    all_to_all x1, waiting for transfers between devices, body(): lax.all_to_all(send_tag, 'ctx', split_axis=0, concat_axis=0, tiled=True)  3.61 us
  transfers between devices with their start and end apart: 7, of which 4 were waited for; matrix products, arithmetic and copies ran while one was open for 9% of the time, Pallas kernels for 0%

commit v1 on v0

v1 whole, which is shorter than its diff:
```python
import functools

import jax
import jax.numpy as jnp
from jax import lax
from jax.experimental import pallas as pl
from jax.experimental.pallas import tpu as pltpu
from jax.sharding import PartitionSpec as P

NEG_FILL = -1e30
MESH = pl.DeviceIdType.MESH


def each(low, high, step):
    if high - low <= 8:
        for i in range(low, high):
            step(i)
    else:
        lax.fori_loop(low, high, lambda i, carry: (step(i), carry)[1], 0)


def dot(a, b, ca, cb):
    return lax.dot_general(
        a, b, (((ca,), (cb,)), ((), ())), preferred_element_type=jnp.float32
    )


def kernel(
    cfg, q_hbm, do_hbm, o_hbm, kv_ref, info_ref, dq_out, dk_out, dv_out,
    q_buf, do_buf, o_buf, kv_buf, info_buf, bias, send_mat, pick_mat, delta,
    scores, acc, dq_send, dq_recv, dkv_send, dkv_recv,
    load_sem, kv_ssem, kv_rsem, info_ssem, info_rsem, dq_ssem, dq_rsem,
    dkv_ssem, dkv_rsem,
):
    dp_n, ctx_n, head_n, back, chunk, block_len = cfg
    rows, width = q_buf.shape
    hd = kv_ref.shape[-1]
    piece = kv_ref.shape[2]
    pairs = dq_send.shape[0]
    blk_pad = dq_send.shape[2]
    wide = dq_send.shape[3]
    per_pair = wide // hd
    scale_val = hd ** (-0.5)
    chunks = (back + 1) * rows // chunk
    dp, ctx, head = lax.axis_index("dp"), lax.axis_index("ctx"), lax.axis_index("head")
    cols = dp_n * head_n
    my_col = dp * head_n + head
    my_piece = head * dp_n + dp

    loads = [
        pltpu.make_async_copy(src, dst, load_sem.at[i])
        for i, (src, dst) in enumerate(((q_hbm, q_buf), (do_hbm, do_buf), (o_hbm, o_buf)))
    ]
    for load in loads:
        load.start()

    barrier = pltpu.get_barrier_semaphore()
    everyone = dp_n * ctx_n * head_n
    me = (dp * ctx_n + ctx) * head_n + head

    def greet(k):
        t = lax.rem(me + k, everyone)
        pl.semaphore_signal(
            barrier, inc=1,
            device_id={"dp": t // (ctx_n * head_n), "ctx": lax.rem(t // head_n, ctx_n), "head": lax.rem(t, head_n)},
            device_id_type=MESH,
        )

    lax.fori_loop(1, everyone, lambda k, c: (greet(k), c)[1], 0)

    kv_buf[:, pl.ds(pl.multiple_of(my_piece * piece, piece), piece), :] = kv_ref[my_col]
    info_buf[ctx] = info_ref[...]
    for_missing = lambda s: pl.when(ctx < s)(
        lambda: kv_buf.__setitem__(
            (slice(None), pl.ds(pl.multiple_of(s * rows, rows), rows), slice(None)),
            jnp.zeros((2, rows, hd), kv_buf.dtype),
        )
    )
    each(1, back + 1, for_missing)
    pl.semaphore_wait(barrier, everyone - 1)

    def info_copy(d):
        return pltpu.make_async_remote_copy(
            src_ref=info_ref, dst_ref=info_buf.at[ctx],
            send_sem=info_ssem.at[d], recv_sem=info_rsem.at[d],
            device_id={"ctx": lax.rem(ctx + d, ctx_n)}, device_id_type=MESH,
        )

    def kv_copy(s, k, target_ctx):
        t = lax.rem(my_col + k, cols)
        return pltpu.make_async_remote_copy(
            src_ref=kv_ref.at[t],
            dst_ref=kv_buf.at[:, pl.ds(pl.multiple_of(s * rows + my_piece * piece, piece), piece), :],
            send_sem=kv_ssem.at[s, k], recv_sem=kv_rsem.at[s, k],
            device_id={"dp": t // head_n, "ctx": target_ctx, "head": lax.rem(t, head_n)}, device_id_type=MESH,
        )

    def kv_start(s):
        def go():
            for k in range(cols):
                if isinstance(s, int) and s == 0 and k == 0:
                    continue
                kv_copy(s, k, lax.rem(ctx + s, ctx_n)).start()
        pl.when(ctx + s < ctx_n)(go)

    def kv_wait(s):
        def go():
            for k in range(cols):
                if isinstance(s, int) and s == 0 and k == 0:
                    continue
                frm = lax.rem(my_col + cols - k, cols)
                place = lax.rem(frm, head_n) * dp_n + frm // head_n
                pltpu.make_async_copy(
                    kv_ref.at[0],
                    kv_buf.at[:, pl.ds(pl.multiple_of(s * rows + place * piece, piece), piece), :],
                    kv_rsem.at[s, k],
                ).wait()
        pl.when(ctx >= s)(go)

    def kv_sent(s):
        def go():
            for k in range(cols):
                if isinstance(s, int) and s == 0 and k == 0:
                    continue
                kv_copy(s, k, lax.rem(ctx + s, ctx_n)).wait_send()
        pl.when(ctx + s < ctx_n)(go)

    each(1, ctx_n, lambda d: info_copy(d).start())
    kv_start(0)
    each(1, back + 1, kv_start)

    for load in loads:
        load.wait()

    def stacked(buf, p):
        return jnp.concatenate(
            [buf[:, (p * per_pair + i) * hd:(p * per_pair + i + 1) * hd] for i in range(per_pair)], axis=0
        )

    for p in range(pairs):
        prod = stacked(do_buf, p).astype(jnp.float32) * stacked(o_buf, p).astype(jnp.float32)
        delta[p] = jnp.sum(prod.T, axis=0, keepdims=True)

    tok = lax.broadcasted_iota(jnp.int32, (blk_pad, rows), 1)
    sub = lax.broadcasted_iota(jnp.int32, (blk_pad, rows), 0)
    same_row = lax.rem(tok, block_len) == sub

    def fill_send(p):
        hit = jnp.broadcast_to(info_ref[1:2, :], (blk_pad, rows)) == p
        at = pl.multiple_of(p * blk_pad, blk_pad)
        send_mat[pl.ds(at, blk_pad), :] = jnp.where(hit & same_row, 1.0, 0.0).astype(send_mat.dtype)

    each(0, ctx_n, fill_send)
    each(1, ctx_n, lambda d: info_copy(d).wait_recv())

    def fill_pick(p):
        hit = jnp.broadcast_to(info_buf[p, 1:2, :], (blk_pad, rows)) == ctx
        at = pl.multiple_of(p * blk_pad, blk_pad)
        pick_mat[pl.ds(at, blk_pad), :] = jnp.where(hit & same_row, 1.0, 0.0).astype(pick_mat.dtype)

    each(0, ctx_n, fill_pick)
    my_doc = jnp.broadcast_to(info_ref[0:1, :], (rows, rows)).astype(jnp.float32)
    key_at = lax.broadcasted_iota(jnp.int32, (rows, rows), 0)
    query_at = lax.broadcasted_iota(jnp.int32, (rows, rows), 1)

    def fill_bias(s):
        src = lax.rem(ctx + ctx_n - s, ctx_n)
        key_doc = jnp.broadcast_to(info_buf[src, 0:1, :], (rows, rows)).astype(jnp.float32).T
        first = jnp.where(ctx >= s, key_at - s * rows, rows)
        seen = (key_doc == my_doc) & (first <= query_at)
        bias[pl.ds(pl.multiple_of(s * rows, rows), rows), :] = jnp.where(seen, 0.0, NEG_FILL)

    each(0, back + 1, fill_bias)
    kv_wait(0)
    each(1, back + 1, kv_wait)

    def dq_copy(p, d):
        t = lax.rem(ctx + d, ctx_n)
        return pltpu.make_async_remote_copy(
            src_ref=dq_send.at[p, t], dst_ref=dq_recv.at[p, ctx],
            send_sem=dq_ssem.at[p, d], recv_sem=dq_rsem.at[p, d],
            device_id={"ctx": t}, device_id_type=MESH,
        )

    def span(i):
        return pl.ds(pl.multiple_of(i * chunk, chunk), chunk)

    def loop(step, start):
        return step(0, start) if chunks == 1 else lax.fori_loop(0, chunks, step, start)

    for p in range(pairs):
        q_p, do_p = stacked(q_buf, p), stacked(do_buf, p)
        delta_p = delta[p]

        def raw(i, peak):
            s = dot(kv_buf[0, span(i), :], q_p, 1, 1) * scale_val
            s = s + jnp.concatenate([bias[span(i), :]] * per_pair, axis=1)
            scores[span(i), :] = s
            return jnp.maximum(peak, jnp.max(s, axis=0, keepdims=True))

        peak = loop(raw, jnp.full((1, wide), NEG_FILL, jnp.float32))

        def weigh(i, total):
            e = jnp.exp(scores[span(i), :] - peak)
            scores[span(i), :] = e
            return total + jnp.sum(e, axis=0, keepdims=True)

        share = 1.0 / loop(weigh, jnp.zeros((1, wide), jnp.float32))

        def grads(i, dq_sum):
            probs = scores[span(i), :] * share
            dprob = dot(kv_buf[1, span(i), :], do_p, 1, 1)
            dscore = (probs * (dprob - delta_p) * scale_val).astype(jnp.bfloat16)
            dk = dot(dscore, q_p, 1, 0)
            dv = dot(probs.astype(jnp.bfloat16), do_p, 1, 0)
            if p > 0:
                dk = dk + acc[0, span(i), :]
                dv = dv + acc[1, span(i), :]
            acc[0, span(i), :] = dk
            acc[1, span(i), :] = dv
            return dq_sum + dot(kv_buf[0, span(i), :], dscore, 0, 0)

        dq_t = loop(grads, jnp.zeros((hd, wide), jnp.float32)).astype(jnp.bfloat16)
        for i in range(per_pair):
            out = dot(send_mat[...], dq_t[:, i * rows:(i + 1) * rows], 1, 1).astype(jnp.bfloat16)
            dq_send[p, :, :, i * hd:(i + 1) * hd] = out.reshape(ctx_n, blk_pad, hd)
        each(1, ctx_n, lambda d: dq_copy(p, d).start())

    def dkv_copy(s):
        return pltpu.make_async_remote_copy(
            src_ref=dkv_send.at[s], dst_ref=dkv_recv.at[s],
            send_sem=dkv_ssem.at[s], recv_sem=dkv_rsem.at[s],
            device_id={"ctx": lax.rem(ctx + ctx_n - s, ctx_n)}, device_id_type=MESH,
        )

    def dkv_start(s):
        def go():
            at = pl.ds(pl.multiple_of(s * rows, rows), rows)
            dkv_send[s] = acc[:, at, :].astype(dkv_send.dtype)
            dkv_copy(s).start()
        pl.when(ctx >= s)(go)

    each(1, back + 1, dkv_start)

    for p in range(pairs):
        dq_recv[p, ctx] = dq_send[p, ctx]
        each(1, ctx_n, lambda d: dq_copy(p, d).wait_recv())
        parts = dq_recv[p].reshape(ctx_n * blk_pad, wide)
        dq_out[:, p * wide:(p + 1) * wide] = dot(pick_mat[...], parts, 0, 0).astype(dq_out.dtype)

    def dkv_add(s):
        def go():
            dkv_copy(s).wait_recv()
            acc[:, 0:rows, :] = acc[:, 0:rows, :] + dkv_recv[s].astype(jnp.float32)
        pl.when(ctx + s < ctx_n)(go)

    each(1, back + 1, dkv_add)
    dk_out[...] = acc[0, 0:rows, :].astype(dk_out.dtype)
    dv_out[...] = acc[1, 0:rows, :].astype(dv_out.dtype)

    kv_sent(0)
    each(1, back + 1, kv_sent)
    each(1, ctx_n, lambda d: info_copy(d).wait_send())
    for p in range(pairs):
        each(1, ctx_n, lambda d: dq_copy(p, d).wait_send())
    each(1, back + 1, lambda s: pl.when(ctx >= s)(lambda: dkv_copy(s).wait_send()))


def body(sizes, queries, keys, values, outputs, grad_out, doc_ids, owner):
    dp_n, ctx_n, head_n = sizes
    rows, _, width = queries.shape
    piece, _, hd = keys.shape
    per_device = owner.shape[0]
    block_len = rows // per_device
    blk_pad = max(block_len, 16)
    group = width // hd
    per_pair = min(2, group)
    pairs, wide = group // per_pair, per_pair * hd
    reach = rows * ctx_n // 2
    back = min(ctx_n - 1, (reach - 1 + rows - 1) // rows)
    take = max(n for n in range(1, 6) if (back + 1) % n == 0)
    keys_seen = (back + 1) * rows

    kv = jnp.transpose(jnp.stack([keys, values]), (2, 0, 1, 3))
    info = jnp.concatenate(
        [doc_ids[None], jnp.repeat(owner, block_len)[None], jnp.zeros((6, rows), jnp.int32)]
    )
    cols = dp_n * head_n
    any_space = pl.BlockSpec(memory_space=pl.ANY)
    vmem = pl.BlockSpec(memory_space=pltpu.VMEM)
    bf16, f32 = jnp.bfloat16, jnp.float32
    dma = pltpu.SemaphoreType.DMA
    outs = pl.pallas_call(
        functools.partial(kernel, (dp_n, ctx_n, head_n, back, take * rows, block_len)),
        out_shape=(
            jax.ShapeDtypeStruct((rows, width), bf16),
            jax.ShapeDtypeStruct((rows, hd), bf16),
            jax.ShapeDtypeStruct((rows, hd), bf16),
        ),
        in_specs=[any_space] * 3 + [vmem] * 2,
        out_specs=(vmem, vmem, vmem),
        scratch_shapes=[
            pltpu.VMEM((rows, width), bf16),
            pltpu.VMEM((rows, width), bf16),
            pltpu.VMEM((rows, width), bf16),
            pltpu.VMEM((2, keys_seen, hd), bf16),
            pltpu.VMEM((ctx_n,) + info.shape, jnp.int32),
            pltpu.VMEM((keys_seen, rows), f32),
            pltpu.VMEM((ctx_n * blk_pad, rows), bf16),
            pltpu.VMEM((ctx_n * blk_pad, rows), bf16),
            pltpu.VMEM((pairs, 1, wide), f32),
            pltpu.VMEM((keys_seen, wide), f32),
            pltpu.VMEM((2, keys_seen, hd), f32),
            pltpu.VMEM((pairs, ctx_n, blk_pad, wide), bf16),
            pltpu.VMEM((pairs, ctx_n, blk_pad, wide), bf16),
            pltpu.VMEM((back + 1, 2, rows, hd), bf16),
            pltpu.VMEM((back + 1, 2, rows, hd), bf16),
            dma((3,)),
            dma((back + 1, cols)), dma((back + 1, cols)),
            dma((ctx_n,)), dma((ctx_n,)),
            dma((pairs, ctx_n)), dma((pairs, ctx_n)),
            dma((back + 1,)), dma((back + 1,)),
        ],
        compiler_params=pltpu.CompilerParams(
            collective_id=0, has_side_effects=True, vmem_limit_bytes=40 * 2**20
        ),
    )(*(a.reshape(rows, width) for a in (queries, grad_out, outputs)), kv, info)
    return tuple(out[:, None, :] for out in outs)


def solution(mesh):
    placed = (
        P("ctx", ("dp", "head"), None),
        P(("ctx", "head", "dp"), None, None),
        P(("ctx", "head", "dp"), None, None),
        P("ctx", ("dp", "head"), None),
        P("ctx", ("dp", "head"), None),
        P("ctx"),
        P("ctx"),
    )
    sizes = tuple(mesh.shape[name] for name in ("dp", "ctx", "head"))
    return jax.shard_map(
        functools.partial(body, sizes),
        mesh=mesh,
        in_specs=placed,
        out_specs=(P("ctx", ("dp", "head"), None),) * 3,
        check_vma=False,
    )
```

time: 129 us -> 45.5 us (0.35)
  blocking collectives: 41 us -> 0 us
  Pallas kernels: 0 us -> 38.3 us
  waiting for transfers between devices: 27.5 us -> 0 us
  starting transfers between devices: 23.4 us -> 0 us
  between operations: 14.2 us -> 0.68 us
  local copies, waits for them, and re-layouts: 12.7 us -> 5.5 us
  matrix products: 3.6 us -> 0 us
  loops' own time: 2.55 us -> 0 us
  other arithmetic: 2.93 us -> 0.74 us
    all_gather x3 -> x0, blocking collectives: 41 us -> none  [the longest x1 14.2 us: body(): lax.all_gather(near_values, 'ctx', axis=0, tiled=True)]
    pallas_call x0 -> x1, Pallas kernels: none -> 38.3 us  [body(): pl.pallas_call(functools.partial(kernel, (dp_n, ctx_n, head_n, back, take...]
    all_to_all x6 -> x0, waiting for transfers between devices: 27.5 us -> none  [the longest x1 20.5 us: body(): lax.all_to_all(jnp.einsum('pj,jbgw->pbgw', send_mat, blocks, preferred_el...]
    all_to_all x6 -> x0, starting transfers between devices: 23.3 us -> none  [the longest x1 5.83 us: body(): lax.all_to_all(send_tag, 'ctx', split_axis=0, concat_axis=0, tiled=True)]
    dot_general x8 -> x0, matrix products: 3.6 us -> none  [the longest x2 1.01 us: raw_scores(): jnp.einsum('rgid,kgd->girk', q_heads, key_block, preferred_element_type=j...]
    convert_element_type x5 -> x0, local copies, waits for them, and re-layouts: 3.27 us -> none  [the longest x1 1.09 us: body(): jnp.einsum('pj,jbgw->pbgw', send_mat, blocks, preferred_element_type=jnp....]
    another operation x6 -> x0, loops' own time: 2.55 us -> none  [the longest x1 1.19 us: body(): lax.fori_loop(0, total_len // key_step, visit_all, (dq_zero, key_zero))]
    all_to_all x3 -> x0, local copies, waits for them, and re-layouts: 1.92 us -> none  [the longest x1 0.68 us: body(): lax.all_to_all(send_tag, 'ctx', split_axis=0, concat_axis=0, tiled=True)]
  transfers between devices with their start and end apart: 7 -> 0, of which waited for: 4 -> 0; matrix products, arithmetic and copies ran while one was open for 9% -> 0% of each run, Pallas kernels for 0% -> 0%
where the time goes in v1:
time: 45.5 us; the launch traced here: 45.2 us
  Pallas kernels  38.3 us (84%)
  local copies, waits for them, and re-layouts  5.5 us (12%)
  other arithmetic  0.74 us (2%)
  between operations  0.68 us (1%)
    pallas_call x1, Pallas kernels, body(): pl.pallas_call(functools.partial(kernel, (dp_n, ctx_n, head_n, back, take...  38.3 us
    unnamed x9, local copies, waits for them, and re-layouts  3.83 us

profile of v1, /device:TPU:0, one launch (start us, length us, event | category | flops | bytes accessed | tf_op | source)
XLA Modules:
  0.0 45.2 jit_solution(8188938774359792627)
XLA Ops:
  0.6 0.0 copy-start
  0.6 0.1 pad.2.clone
  0.7 0.7 %broadcast_in_dim.19 = s32[4,32]{1,0:T(4,128)S(1)} broadcast(s32[4]{0:T(128)} %param.13), dimensions={0} | broadcast | bytes 528 | tf_op jit(solution)/shard_map/broadcast_in_dim | solution.py:286
  1.4 0.1 broadcast_in_dim_reshape.3
  1.5 0.7 %add_add_fusion.info_ref = s32[8,128]{1,0:T(8,128)S(1)} fusion(s32[1,128]{1,0:T(1,128)S(1)} %broadcast_in_dim_reshape.3, s32[1,128]{1,0:T(1,128)} %bitcast.19, s32[8]{0:T(128)S(1)} %pad.2.clone), kind=kLoop, calls=%fused_computation.3 | loop fusion | flops 2048 | bytes 5152 | tf_op jit(solution)/shard_map/concatenate | solution.py:285
  2.3 0.8 %copy_bitcast_fusion = (bf16[1,32,4,128]{3,1,0,2:T(8,128)(2,1)S(1)}, bf16[1,32,4,128]{3,1,0,2:T(8,128)(2,1)S(1)}) fusion(bf16[32,4,128]{2,1,0:T(4,128)(2,1)} %param.9, bf16[32,4,128]{2,1,0:T(4,128)(2,1)} %param.8), kind=kLoop, calls=%fused_computation.1 | loop fusion | bytes 131072 | tf_op jit(solution)/shard_map/stack | solution.py:284
  3.1 0.0 copy-done
  3.1 0.0 copy-start.1
  3.1 0.9 %copy-done.1 = bf16[128,1,1024]{2,0,1:T(8,128)(2,1)S(1)} copy-done((bf16[128,1,1024]{2,0,1:T(8,128)(2,1)S(1)}, bf16[128,1,1024]{2,0,1:T(8,128)(2,1)}, u32[]{:S(2)}) %copy-start.1) | copy-done | bytes 262168
  4.0 0.0 copy-start.2
  4.0 0.9 %copy-done.2 = bf16[128,1,1024]{2,0,1:T(8,128)(2,1)S(1)} copy-done((bf16[128,1,1024]{2,0,1:T(8,128)(2,1)S(1)}, bf16[128,1,1024]{2,0,1:T(8,128)(2,1)}, u32[]{:S(2)}) %copy-start.2) | copy-done | bytes 262168
  5.0 38.3 %shard_map.94 = (bf16[128,1024]{1,0:T(8,128)(2,1)S(1)}, bf16[128,128]{1,0:T(8,128)(2,1)S(1)}, bf16[128,128]{1,0:T(8,128)(2,1)S(1)}) custom-call(bf16[128,1024]{1,0:T(8,128)(2,1)S(1)} %bitcast.13, bf16[128,1024]{1,0:T(8,128)(2,1)S(1)} %bitcast.14, bf16[128,1024]{1,0:T(8,128)(2,1)S(1)} %bitcast.15, bf16[4,2,32,128]{3,2,1,0:T(8,128)(2,1)S(1)} %maximum_bitcast_fusion.kv_ref, ...), custom_call_target="tpu_custom_call" | custom-call | tf_op jit(solution)/shard_map/pallas_call | solution.py:293
  43.2 0.7 %copy.17 = bf16[128,1,1024]{2,0,1:T(8,128)(2,1)} copy(bf16[128,1,1024]{2,0,1:T(8,128)(2,1)S(1)} %bitcast.16) | data formatting | bytes 524288
  44.0 0.6 %copy.18 = bf16[128,1,128]{2,0,1:T(8,128)(2,1)} copy(bf16[128,1,128]{2,0,1:T(8,128)(2,1)S(1)} %bitcast.18) | data formatting | bytes 65536
  44.6 0.6 %copy.19 = bf16[128,1,128]{2,0,1:T(8,128)(2,1)} copy(bf16[128,1,128]{2,0,1:T(8,128)(2,1)S(1)} %bitcast.17) | data formatting | bytes 65536
  (2 shorter events, 0.0 us)
Async XLA Ops:
  0.6 2.4 %copy-start = (bf16[128,1,1024]{2,0,1:T(8,128)(2,1)S(1)}, bf16[128,1,1024]{2,0,1:T(8,128)(2,1)}, u32[]{:S(2)}) copy-start(bf16[128,1,1024]{2,0,1:T(8,128)(2,1)} %param.7) | copy-start | bytes 786436
  3.1 1.0 %copy-start.1 = (bf16[128,1,1024]{2,0,1:T(8,128)(2,1)S(1)}, bf16[128,1,1024]{2,0,1:T(8,128)(2,1)}, u32[]{:S(2)}) copy-start(bf16[128,1,1024]{2,0,1:T(8,128)(2,1)} %param.11) | copy-start | bytes 786436
  4.0 0.9 %copy-start.2 = (bf16[128,1,1024]{2,0,1:T(8,128)(2,1)S(1)}, bf16[128,1,1024]{2,0,1:T(8,128)(2,1)}, u32[]{:S(2)}) copy-start(bf16[128,1,1024]{2,0,1:T(8,128)(2,1)} %param.10) | copy-start | bytes 786436
